TPU v7x, 32 devices: a whole 2x2x4 slice. The times are simulated.
32 devices in a mesh: dp: 8 (over z, core), shard: 4 (over y, x).
Axes of the slice: x: 2, y: 2, z: 4, core: 2. Of those that a mesh axis runs over, the one named last changes fastest.
Arguments:
- queries: float32 [16384, 256], P(('dp', 'shard'))
- items: float32 [81920, 256], P('shard')
- positive: int32 [16384], P(('dp', 'shard')), may hold values from 0 to 81919
- tile_ids: int32 [32, 4, 3], P(('dp', 'shard')), may hold values from 0 to 39, as said below
- counts: int32 [32, 4], P(('dp', 'shard')), may hold values from 1 to 3, as said below
Outputs:
- loss: float32 [16384], P(('dp', 'shard'))
- query_grad: float32 [16384, 256], P(('dp', 'shard'))
- item_grad: float32 [81920, 256], P(('shard', 'dp'))
Inputs may be any that keep to these rules, and one draw needn't show every extreme that they name: `tile_ids`: within one block and shard the 3 entries are distinct; only the first counts of them are visited. `counts`: every block visits exactly 3 tiles on at least one shard.
All inputs are finite; a program needn't handle non-finite values.
Results may differ from a plain program's by a relative error of at most 0.0003.
Values sent between devices are 32-bit elements; how exact they have to be, the bound alone decides.
No kernel may reach another device: no remote copies, remote signals or barrier semaphores. Data moves between devices by JAX's collectives and lax.ppermute only.
A program may use at most 192 MiB of HBM per device.

v0:
```python
import functools

import jax
import jax.numpy as jnp
from jax import lax
from jax.experimental import pallas as pl
from jax.experimental.pallas import tpu as pltpu
from jax.sharding import PartitionSpec as P

TILE = 512
KMAX = 3
EXTRA = 8
LOADS = 8
GATHER = 8
STEP = 4
STAT = 4
MIB = 1024 * 1024
VMEM_LIMIT = 10 * MIB

very_low = -1e30
high, highest = lax.Precision.HIGH, lax.Precision.HIGHEST

smem = pl.BlockSpec(memory_space=pltpu.SMEM)
vmem = pl.BlockSpec(memory_space=pltpu.VMEM)
anywhere = pl.BlockSpec(memory_space=pl.ANY)
hbm = pl.BlockSpec(memory_space=pltpu.HBM)


def dot(a, b, dims=((1,), (0,)), precision=high):
    return lax.dot_general(a, b, (dims, ((), ())), precision=precision, preferred_element_type=jnp.float32)


def halves(x):
    upper = x.astype(jnp.bfloat16)
    return upper, (x - upper.astype(jnp.float32)).astype(jnp.bfloat16)


def dot3(a, b, dims=((1,), (0,))):
    def one(i, j):
        return lax.dot_general(a[i], b[j], (dims, ((), ())), preferred_element_type=jnp.float32)

    return (one(0, 1) + one(1, 0)) + one(0, 0)


def cost(us):
    return pl.CostEstimate(flops=0, bytes_accessed=int(us * 3.0e6), transcendentals=0)


def pack_kernel(step, ids_ref, counts_ref, q_ref, pos_ref, out_ref, sem):
    rows, width = q_ref.shape
    get_q = pltpu.make_async_copy(q_ref, out_ref.at[:rows], sem)
    get_q.start()
    out_ref[rows : rows + EXTRA, :] = jnp.zeros((EXTRA, width), jnp.float32)
    row = pos_ref[...].astype(jnp.float32)
    col = jnp.broadcast_to(row, (8, rows)).T[:, 0:1]
    at_row = lax.broadcasted_iota(jnp.int32, (rows, rows), 1)
    at_col = lax.broadcasted_iota(jnp.int32, (rows, rows), 0)
    before = (row < col) | ((row == col) & (at_row < at_col))
    rank = jnp.sum(before.astype(jnp.float32), axis=1, keepdims=True)
    placed = rank == at_row.astype(jnp.float32)
    sorted_pos = jnp.sum(jnp.where(placed, col, 0.0), axis=0, keepdims=True)
    sorted_at = jnp.sum(jnp.where(placed, at_col.astype(jnp.float32), 0.0), axis=0, keepdims=True)
    starts = lax.broadcasted_iota(jnp.int32, (rows, width), 1).astype(jnp.float32) * step
    bounds = jnp.sum((col < starts).astype(jnp.float32), axis=0, keepdims=True)
    lane = lax.broadcasted_iota(jnp.int32, (1, width), 1)
    lists = jnp.zeros((1, width), jnp.int32)
    n = counts_ref.shape[1]
    for i in range(n * KMAX):
        lists = jnp.where(lane == i, ids_ref[0, i // KMAX, i % KMAX], lists)
    for i in range(n):
        lists = jnp.where(lane == n * KMAX + i, counts_ref[0, i], lists)
    per = rows // width
    out_ref[rows + 3 * per : rows + 3 * per + 1, :] = lists.astype(jnp.float32)
    out_ref[rows + 3 * per + 1 : rows + 3 * per + 2, :] = bounds
    for first, values in ((0, row), (per, sorted_pos), (2 * per, sorted_at)):
        for i in range(per):
            out_ref[rows + first + i : rows + first + i + 1, :] = values[:, i * width : (i + 1) * width]
    get_q.wait()


def pack(queries, positive, tile_ids, counts, step):
    rows, width = queries.shape
    return pl.pallas_call(
        functools.partial(pack_kernel, float(step)),
        out_shape=jax.ShapeDtypeStruct((rows + EXTRA, width), jnp.float32),
        in_specs=[smem, smem, hbm, vmem],
        out_specs=vmem,
        scratch_shapes=[pltpu.SemaphoreType.DMA],
        compiler_params=pltpu.CompilerParams(vmem_limit_bytes=VMEM_LIMIT),
        cost_estimate=cost(2),
        name="pack",
    )(tile_ids, counts, queries, positive.reshape(1, rows))


class Lists:
    def __init__(self, ref, rows, shard_at, n_shard):
        self.ref, self.rows, self.shard_at, self.n_shard = ref, rows, shard_at, n_shard
        self.width = ref.shape[2]
        self.per = rows // self.width
        self.shift = self.width.bit_length() - 1

    def entry(self, b, first, i):
        return self.ref[b, first + (i >> self.shift), i & (self.width - 1)]

    def sorted_pos(self, b, i):
        return self.entry(b, self.per, i)

    def place(self, b, i):
        return self.entry(b, 2 * self.per, i)

    def tile(self, b, k):
        return self.ref[b, 3 * self.per, self.shard_at * KMAX + k]

    def count(self, b):
        return self.ref[b, 3 * self.per, self.n_shard * KMAX + self.shard_at]

    def bound(self, b, i):
        return self.ref[b, 3 * self.per + 1, i]


def swap(x, axis, bits):
    return lax.ppermute(x, axis, [(i, i ^ bits) for i in range(lax.axis_size(axis))])


def none(*xs):
    return sum(jnp.minimum(jnp.abs(x[(0,) * x.ndim]), 0.0) for x in xs)


def together(*xs):
    return lax.optimization_barrier(xs)


def stats_kernel(n, n_before, n_shard, loads, at, *refs):
    msgs, refs = refs[:n], refs[n:]
    befores, refs = refs[:n_before], refs[n_before:]
    source, acc_ref, chosen_ref, stat_ref, refs = refs[0], refs[1], refs[2], refs[3], refs[4:]
    items = source
    if loads:
        items, refs = refs[0], refs[1:]
    if loads:
        tiles, tile_sems, refs = refs[0], refs[1], refs[2:]
    q_ref, rowbuf, whole, lists_ref, sems, load_sems = refs
    rows = q_ref.shape[1] - EXTRA
    width = q_ref.shape[2]
    per = rows // width
    lists = Lists(lists_ref, rows, at[0], n_shard)
    base, local_rows = at[1], items.shape[0]
    chunk = local_rows // LOADS
    get_lists = pltpu.make_async_copy(whole, lists_ref, sems.at[1, 0])

    def get_q(j):
        return pltpu.make_async_copy(msgs[j], q_ref.at[j], sems.at[0, j])

    def get_items(i):
        part = pl.ds(i * chunk, chunk)
        return pltpu.make_async_copy(source.at[part], items.at[part], load_sems.at[i])

    def get_tile(k):
        start = pl.multiple_of(lists.tile(0, k) * TILE, TILE)
        return pltpu.make_async_copy(source.at[pl.ds(start, TILE)], tiles.at[k], tile_sems.at[k])

    for j in range(n):
        get_q(j).start()
    first = 0
    for before in befores:
        stat_ref[first : first + before.shape[0]] = before[...]
        first += before.shape[0]
    for j in range(n):
        get_q(j).wait()
    whole[...] = q_ref[:, rows:, :].astype(jnp.int32)
    get_lists.start()
    get_lists.wait()
    if loads:

        @pl.loop(0, lists.count(0))
        def _(k):
            get_tile(k).start()

        for i in range(LOADS):
            get_items(i).start()

    @pl.loop(0, n)
    def _(b):
        q_t = q_ref[b, :rows, :].T
        q_halves = halves(q_t)
        acc_ref[b] = jnp.zeros(acc_ref.shape[1:], jnp.float32)

        def visit(k, carry):
            top, total = carry
            if loads:
                get_tile(k).wait()
                tile = tiles[k]
            else:
                tile = items[pl.ds(pl.multiple_of(lists.tile(b, k) * TILE, TILE), TILE), :]
            logits = dot3(halves(tile), q_halves)
            new_top = jnp.maximum(top, jnp.max(logits, axis=0, keepdims=True))
            prob = jnp.exp(logits - new_top)
            scale = jnp.exp(top - new_top)
            total = total * scale + jnp.sum(prob, axis=0, keepdims=True)
            acc_ref[b] = acc_ref[b] * scale + dot(tile.T, prob)
            return new_top, total

        start = (jnp.full((1, rows), very_low, jnp.float32), jnp.zeros((1, rows), jnp.float32))
        top, total = lax.fori_loop(0, lists.count(b), visit, start)

        if loads:
            for i in range(LOADS):
                get_items(i).wait()
        rowbuf[...] = jnp.zeros(rowbuf.shape, jnp.float32)
        low, high_end = lists.bound(b, at[0] * at[4]), lists.bound(b, (at[0] + 1) * at[4])

        @pl.loop(0, (high_end - low + GATHER - 1) // GATHER)
        def _(c):
            entries = [jnp.minimum(low + c * GATHER + u, high_end - 1) for u in range(GATHER)]
            got = [items[pl.ds(lists.sorted_pos(b, i) - base, 1), :] for i in entries]
            for i, row in zip(entries, got):
                rowbuf[pl.ds(lists.place(b, i), 1), :] = row

        chosen = rowbuf[...].T
        chosen_ref[b] = chosen
        pos = jnp.concatenate([q_ref[b, rows + i : rows + i + 1, :] for i in range(per)], axis=1).astype(jnp.int32)
        offset = pos - base
        inside = (offset >= 0) & (offset < local_rows)
        plogit = jnp.sum(q_t * chosen, axis=0, keepdims=True)
        new_top = jnp.maximum(top, jnp.where(inside, plogit, very_low))
        total = total * jnp.exp(top - new_top) + jnp.where(inside, jnp.exp(plogit - new_top), 0.0)
        stat_ref[first + b, 0:1, :] = top
        stat_ref[first + b, 1:2, :] = new_top + jnp.log(total)
        stat_ref[first + b, 2:3, :] = jnp.where(inside, plogit, 0.0)
        stat_ref[first + b, 3:4, :] = jnp.where(inside, 1.0, 0.0)


def stats(messages, befores, items, at, loads):
    n = len(messages)
    rows, width = messages[0].shape[0] - EXTRA, messages[0].shape[1]
    total = n + sum(b.shape[0] for b in befores)
    sums = jax.ShapeDtypeStruct((n, width, rows), jnp.float32)
    held = [pltpu.VMEM(items.shape, jnp.float32)] if loads else []
    return pl.pallas_call(
        functools.partial(stats_kernel, n, len(befores), lax.axis_size("shard"), loads),
        out_shape=(sums, sums, jax.ShapeDtypeStruct((total, STAT, rows), jnp.float32), *held),
        in_specs=[smem] + [anywhere] * n + [vmem] * len(befores) + [hbm if loads else vmem],
        out_specs=(vmem, vmem, vmem, *[vmem] * len(held)),
        scratch_shapes=[
            *([pltpu.VMEM((KMAX, TILE, width), jnp.float32), pltpu.SemaphoreType.DMA((KMAX,))] if loads else []),
            pltpu.VMEM((n, rows + EXTRA, width), jnp.float32),
            pltpu.VMEM((rows, width), jnp.float32),
            pltpu.VMEM((n, EXTRA, width), jnp.int32),
            pltpu.SMEM((n, EXTRA, width), jnp.int32),
            pltpu.SemaphoreType.DMA((2, n)),
            pltpu.SemaphoreType.DMA((LOADS,)),
        ],
        compiler_params=pltpu.CompilerParams(vmem_limit_bytes=VMEM_LIMIT),
        cost_estimate=cost(5 * n),
        name="stats",
    )(at, *messages, *befores, items)


def dq_kernel(n, counts, *refs):
    stat_refs, refs = refs[:n], refs[n:]
    acc_refs, refs = refs[: len(counts)], refs[len(counts) :]
    chosen_refs, refs = refs[: len(counts)], refs[len(counts) :]
    loss_ref, term_ref, even_ref, odd_ref = refs
    b = 0
    for acc_ref, chosen_ref, count in zip(acc_refs, chosen_refs, counts):
        for i in range(count):
            parts = [stat_refs[j][b ^ j, 1:2, :] for j in range(n)]
            top = functools.reduce(jnp.maximum, parts)
            lse = top + jnp.log(sum(jnp.exp(p - top) for p in parts))
            plogit = sum(stat_refs[j][b ^ j, 2:3, :] for j in range(n))
            weight = jnp.exp(plogit - lse) - 1.0
            term_ref[0, b : b + 1, :] = lse
            term_ref[1, b : b + 1, :] = weight
            if b == 0:
                loss_ref[...] = lse - plogit
            own = stat_refs[0]
            share = acc_ref[i] * jnp.exp(own[b, 0:1, :] - lse) + chosen_ref[i] * (weight * own[b, 3:4, :])
            (odd_ref if b % 2 else even_ref)[b // 2] = share.T
            b += 1


def dq_shares(all_stats, accs, chosens):
    n, _, rows = all_stats[0].shape
    width = accs[0].shape[1]
    share = jax.ShapeDtypeStruct((n // 2, rows, width), jnp.float32)
    return pl.pallas_call(
        functools.partial(dq_kernel, n, [a.shape[0] for a in accs]),
        out_shape=(jax.ShapeDtypeStruct((1, rows), jnp.float32), jax.ShapeDtypeStruct((2, n, rows), jnp.float32), share, share),
        compiler_params=pltpu.CompilerParams(vmem_limit_bytes=VMEM_LIMIT),
        cost_estimate=cost(3),
        name="dq",
    )(*all_stats, *accs, *chosens)


def item_kernel(groups, n_shard, n_waits, n_through, is_first, is_last, at, *refs):
    n = sum(size for size, _ in groups)
    weights, refs = refs[: len(groups)], refs[len(groups) :]
    msgs, refs = refs[:n], refs[n + n_waits :]
    lse_refs, refs = refs[: len(groups)], refs[len(groups) :]
    items, refs = refs[0], refs[1 if is_first else 2 :]
    acc, token, refs = refs[0], refs[1], refs[2:]
    if is_first:
        source, items, refs = items, refs[0], refs[1:]
    outs, refs = refs[: 2 * is_last], refs[2 * is_last + n_through :]
    q_ref, lse, whole, lists_ref, sems = refs
    rows, width = q_ref.shape[1] - EXTRA, q_ref.shape[2]
    span_rows = acc.shape[0]
    tiles = span_rows // TILE
    base, first_tile, core = at[1] + at[2] * TILE, at[2], at[3]
    chip = at[0] * at[4] + at[5]
    lists = Lists(lists_ref, rows, at[0], n_shard)
    get_lists = pltpu.make_async_copy(whole, lists_ref, sems.at[1, 0])

    def get_q(j):
        return pltpu.make_async_copy(msgs[j], q_ref.at[j], sems.at[0, j])

    for j in range(n):
        get_q(j).start()
    if is_first:
        start = pl.multiple_of(first_tile * TILE, TILE)
        get_items = pltpu.make_async_copy(source.at[pl.ds(start, span_rows)], items, sems.at[2, 0])
        get_items.start()
        acc[...] = jnp.zeros(acc.shape, jnp.float32)
    token[...] = jnp.zeros(token.shape, jnp.float32)
    for j in range(n):
        get_q(j).wait()
    whole[...] = q_ref[:, rows:, :].astype(jnp.int32)
    get_lists.start()
    get_lists.wait()

    def add_positives(b, weight, first):
        low, top = lists.bound(b, chip), lists.bound(b, chip + 1)

        @pl.loop(0, (top - low + STEP - 1) // STEP)
        def _(c):
            entries = [jnp.minimum(low + c * STEP + u, top - 1) for u in range(STEP)]
            rests = [jnp.where(low + c * STEP + u < top, 1.0, 0.0) for u in range(STEP)]
            heres = [lists.sorted_pos(b, i) - base for i in entries]
            places = [lists.place(b, i) for i in entries]
            olds = [acc[pl.ds(h, 1), :] for h in heres]
            terms = [q_ref[b, pl.ds(p, 1), :] * (weight[1, b - first, p] * r) for p, r in zip(places, rests)]
            for u in range(1, STEP):
                terms[u] = terms[u] + terms[u - 1] * jnp.where(heres[u] == heres[u - 1], 1.0, 0.0)
            for h, old, term in zip(heres, olds, terms):
                acc[pl.ds(h, 1), :] = old + term

    first = 0
    for (size, begin), weight, lse_ref in zip(groups, weights, lse_refs):
        lse[first : first + size, :] = lse_ref[0, begin : begin + size, :]
        pl.loop(first, first + size)(functools.partial(add_positives, weight=weight, first=first - begin))
        first += size

    if is_first:
        get_items.wait()

    @pl.loop(0, n)
    def _(b):
        @pl.loop(0, lists.count(b))
        def _(k):
            tile = lists.tile(b, k) - first_tile

            @pl.when((tile >= 0) & (tile < tiles))
            def _():
                here = pl.ds(pl.multiple_of(tile * TILE, TILE), TILE)
                q = q_ref[b, :rows, :]
                logits = dot3(halves(items[here, :]), halves(q), ((1,), (1,)))
                prob = jnp.exp(logits - lse[pl.ds(b, 1), :])
                acc[here, :] += dot(prob, q)

    if is_last:
        own = span_rows // 2
        mine, other = outs
        put = [
            pltpu.make_async_copy(acc.at[pl.ds(pl.multiple_of((1 - core) * own, 8), own)], other, sems.at[2, 0]),
            pltpu.make_async_copy(acc.at[pl.ds(pl.multiple_of(core * own, 8), own)], mine, sems.at[2, 1]),
        ]
        for p in put:
            p.start()
        for p in put:
            p.wait()


def item_grads(groups, terms, items, acc, span_rows, at, is_last, waits=(), through=()):
    waits = [*waits, *through]
    messages = [m for group, _ in groups for m in group]
    n = len(messages)
    rows, width = messages[0].shape[0] - EXTRA, messages[0].shape[1]
    is_first = acc is None
    half = jax.ShapeDtypeStruct((span_rows // 2, width), jnp.float32)
    chips = pltpu.VMEM((span_rows, width), jnp.float32)
    token = jax.ShapeDtypeStruct((1, 128), jnp.float32)
    more = [chips] if is_first else [half, half] if is_last else []
    carried = [] if is_first else [acc]
    sizes = [(len(group), begin) for group, begin in groups]
    return pl.pallas_call(
        functools.partial(item_kernel, sizes, lax.axis_size("shard"), len(waits), len(through), is_first, is_last),
        out_shape=(chips, token, *more, *[jax.ShapeDtypeStruct(x.shape, x.dtype) for x in through]),
        in_specs=[smem] * (1 + len(groups))
        + [anywhere] * (n + len(waits))
        + [vmem] * len(groups)
        + [hbm if is_first else vmem]
        + [vmem] * len(carried),
        out_specs=(vmem, vmem, *[vmem if is_first else anywhere] * len(more), *[anywhere] * len(through)),
        scratch_shapes=[
            pltpu.VMEM((n, rows + EXTRA, width), jnp.float32),
            pltpu.VMEM((n, rows), jnp.float32),
            pltpu.VMEM((n, EXTRA, width), jnp.int32),
            pltpu.SMEM((n, EXTRA, width), jnp.int32),
            pltpu.SemaphoreType.DMA((3, max(n, 2))),
        ],
        input_output_aliases={
            **({} if is_first else {2 + 2 * len(groups) + n + len(waits): 0}),
            **{1 + len(groups) + n + len(waits) - len(through) + i: 2 + len(more) + i for i in range(len(through))},
        },
        compiler_params=pltpu.CompilerParams(vmem_limit_bytes=VMEM_LIMIT + max(n - 4, 0) * MIB),
        cost_estimate=cost(2 * n),
        name="item_grads",
    )(at, *terms, *messages, *waits, *terms, items, *carried)


def local(queries, items, positive, tile_ids, counts):
    dp_at, shard_at = lax.axis_index("dp"), lax.axis_index("shard")
    n_dp, n_shard = lax.axis_size("dp"), lax.axis_size("shard")
    rows, width = queries.shape
    local_rows = items.shape[0]
    span_rows = 2 * (local_rows // n_dp)
    n_chips = n_dp // 2
    chip_at = dp_at // 2
    at = jnp.stack([shard_at, shard_at * local_rows, chip_at * (span_rows // TILE), dp_at % 2, n_chips, chip_at])
    at = at.astype(jnp.int32)

    def top(j):
        return 1 << (j.bit_length() - 1)

    items = pltpu.with_memory_space_constraint(items, pltpu.HBM)
    queries = pltpu.with_memory_space_constraint(queries, pltpu.HBM)
    message = pack(queries, positive, tile_ids, counts, span_rows)
    own = [message] + [swap(message, "shard", j) for j in (1, 2)]
    straight = [message, None, swap(message, "dp", 4)]
    acc0, chosen0, stat0, held = stats([message], [], items, at, True)

    message, own[1], own[2], stat0 = together(message, own[1], own[2], stat0)
    straight[1] = swap(message, "dp", 2)
    for j in range(3, n_shard):
        own.append(swap(own[j ^ top(j)], "shard", top(j)))
    acc1, chosen1, stat1 = stats(own[1:3], [stat0], held, at, False)

    message, straight[2], stat1, *own[3:] = together(message, straight[2], stat1, *own[3:])
    straight += [swap(message, "dp", 2 * k) for k in range(3, n_chips)]
    far = {2: [straight[2]] + [swap(straight[2], "shard", j) for j in (1, 2)]}
    acc2, chosen2, stat = stats(own[3:], [stat1], held, at, False)

    all_stats = [stat]
    bit = 1
    while bit < n_shard:
        got = swap(jnp.stack(all_stats) if bit > 1 else stat, "shard", bit)
        all_stats += [got[j] for j in range(bit)] if bit > 1 else [got]
        bit *= 2
    all_stats[-1], far[2][1], far[2][2], straight[1], *straight[3:] = together(
        all_stats[-1], far[2][1], far[2][2], straight[1], *straight[3:]
    )
    loss, sent, even, odd = dq_shares(all_stats, [acc0, acc1, acc2], [chosen0, chosen1, chosen2])

    for k in range(3, n_chips):
        far[k] = [straight[k]] + [swap(straight[k], "shard", j) for j in (1, 2)]
    for j in range(3, n_shard):
        far[2].append(swap(far[2][j ^ top(j)], "shard", top(j)))
    grads, token, chip_items, odd = item_grads([(own, 0)], [sent], items, None, span_rows, at, False, through=[odd])
    near = [straight[1], swap(own[1], "dp", 2)]
    early = [token, near[1], *[m for k in range(3, n_chips) for m in far[k][1:]]]
    terms = [sent]
    bit = 1
    while bit < n_chips:
        got = swap(jnp.stack(terms) + none(*early) if bit > 1 else sent, "dp", 2 * bit)
        terms += [got[j] for j in range(bit)] if bit > 1 else [got]
        bit *= 2
    near += [swap(own[j] + none(terms[n_chips - 1]), "dp", 2) for j in range(2, n_shard)]
    for k in range(3, n_chips):
        for j in range(3, n_shard):
            far[k].append(swap(far[k][j ^ top(j)], "shard", top(j)))
    grads, token = item_grads([(far[2], 0)], [terms[2]], chip_items, grads, span_rows, at, False)[:2]

    shares = even + swap(odd, "shard", 1) + none(token)
    half_way = shares
    bit = 2
    while bit < n_shard:
        shares = shares[0::2] + swap(shares[1::2], "shard", bit)
        bit *= 2
    query_grad = shares[0]
    for k in range(3, n_chips - 1):
        grads = item_grads([(far[k], 0)], [terms[k]], chip_items, grads, span_rows, at, False)[0]
    k = n_chips - 1
    most = [(far[k], 0), (near[: n_shard - 1], 0)]
    grads = item_grads(most, [terms[k], terms[1]], chip_items, grads, span_rows, at, False, [half_way])[0]
    rest = [(near[n_shard - 1 :], n_shard - 1)]
    mine, other = item_grads(rest, [terms[1]], chip_items, grads, span_rows, at, True, [query_grad])[2:]
    item_grad = mine + swap(other, "dp", 1)
    return loss.reshape(rows), query_grad, item_grad


def solution(mesh):
    placed = (
        P(("dp", "shard"), None),
        P("shard", None),
        P(("dp", "shard")),
        P(("dp", "shard"), None, None),
        P(("dp", "shard"), None),
    )
    return jax.shard_map(
        local,
        mesh=mesh,
        in_specs=placed,
        out_specs=(P(("dp", "shard")), P(("dp", "shard"), None), P(("shard", "dp"), None)),
        check_vma=False,
    )
```

profile of v0, /device:TPU:0, one launch (start us, length us, event | category | flops | bytes accessed | tf_op | source)
XLA Modules:
  0.0 131.2 jit_solution(1912244276727544486)
XLA Ops:
  0.6 0.8 copy.12.ids_ref
  2.7 1.6 %pack.1.refs_0_.refs_1_ = f32[520,256]{1,0:T(8,128)S(1)} custom-call(s32[1,4,3]{2,1,0:T(4,128)S(1)} %copy.12.ids_ref, s32[1,4]{1,0:T(1,128)S(1)} %copy-done.2, f32[512,256]{1,0:T(8,128)} %q_ref.1, s32[1,512]{1,0:T(1,128)S(1)} %bitcast.30), custom_call_target="tpu_custom_call" | custom-call | bytes 6000000 | tf_op jit(solution)/shard_map/pack/pallas_call | solution.py:83
  4.4 3.0 %collective-permute-start = (f32[520,256]{1,0:T(8,128)S(1)}, f32[520,256]{1,0:T(8,128)S(1)}, u32[]{:S(2)}, u32[]{:S(2)}) collective-permute-start(f32[520,256]{1,0:T(8,128)S(1)} %pack.1.refs_0_.refs_1_), channel_id=1, source_target_pairs={{0,1},{1,0},{2,3},{3,2},{4,5},{5,4},{6,7},{7,6},{8,9},{9,8},{10,11... | collective-permute-start | bytes 1597448 | tf_op jit(solution)/shard_map/ppermute | solution.py:122
  7.4 1.5 %collective-permute-start.1 = (f32[520,256]{1,0:T(8,128)S(1)}, f32[520,256]{1,0:T(8,128)S(1)}, u32[]{:S(2)}, u32[]{:S(2)}) collective-permute-start(f32[520,256]{1,0:T(8,128)S(1)} %pack.1.refs_0_.refs_1_), channel_id=1, source_target_pairs={{0,2},{1,3},{2,0},{3,1},{4,6},{5,7},{6,4},{7,5},{8,10},{9,11},{10,... | collective-permute-start | bytes 1597448 | tf_op jit(solution)/shard_map/ppermute | solution.py:122
  8.9 2.6 %collective-permute-start.2 = (f32[520,256]{1,0:T(8,128)S(1)}, f32[520,256]{1,0:T(8,128)S(1)}, u32[]{:S(2)}, u32[]{:S(2)}) collective-permute-start(f32[520,256]{1,0:T(8,128)S(1)} %pack.1.refs_0_.refs_1_), channel_id=1, source_target_pairs={{0,16},{4,20},{8,24},{12,28},{16,0},{20,4},{24,8},{28,12},{1,17},{... | collective-permute-start | bytes 1597448 | tf_op jit(solution)/shard_map/ppermute | solution.py:122
  11.6 10.4 %stats.3 = (f32[1,256,512]{2,1,0:T(8,128)S(1)}, f32[1,256,512]{2,1,0:T(8,128)S(1)}, f32[1,4,512]{2,1,0:T(4,128)S(1)}, f32[20480,256]{1,0:T(8,128)S(1)}) custom-call(s32[6]{0:T(128)S(1)} %stack.41.at, f32[520,256]{1,0:T(8,128)S(1)} %pack.1.refs_0_.refs_1_, f32[20480,256]{1,0:T(8,128)} %refs_7_.1), custom_call_target="tpu_custom_call" | custom-call | bytes 15000000 | tf_op jit(solution)/shard_map/stats/pallas_call | solution.py:239
  22.0 0.9 collective-permute-start.3
  22.8 1.2 collective-permute-start.8
  24.1 9.6 %stats.4 = (f32[2,256,512]{2,1,0:T(8,128)S(1)}, f32[2,256,512]{2,1,0:T(8,128)S(1)}, f32[3,4,512]{2,1,0:T(4,128)S(1)}) custom-call(s32[6]{0:T(128)S(1)} %stack.41.at, f32[520,256]{1,0:T(8,128)S(1)} %collective-permute-done.refs_0_.refs_2_, f32[520,256]{1,0:T(8,128)S(1)} %collective-permute-done.1.refs_1_.refs_3_, f32[1,4,512]{2,1,0:T(4,128)S(1)} %get-tuple-element.43.refs_2_, ...), custom_call_target="tpu_custom_call" | custom-call | bytes 30000000 | tf_op jit(solution)/shard_map/stats/pallas_call | solution.py:239
  33.7 0.9 collective-permute-done.2.refs_1_
  35.2 0.7 collective-permute-start.6
  35.9 2.7 %collective-permute-start.7 = (f32[520,256]{1,0:T(8,128)S(1)}, f32[520,256]{1,0:T(8,128)S(1)}, u32[]{:S(2)}, u32[]{:S(2)}) collective-permute-start(f32[520,256]{1,0:T(8,128)S(1)} %collective-permute-done.2.refs_1_), channel_id=1, source_target_pairs={{0,2},{1,3},{2,0},{3,1},{4,6},{5,7},{6,4},{7,5},{8,10},{9,11},{10,... | collective-permute-start | bytes 1597448 | tf_op jit(solution)/shard_map/ppermute | solution.py:122
  39.3 6.3 %stats.5 = (f32[1,256,512]{2,1,0:T(8,128)S(1)}, f32[1,256,512]{2,1,0:T(8,128)S(1)}, f32[4,4,512]{2,1,0:T(4,128)S(1)}) custom-call(s32[6]{0:T(128)S(1)} %stack.41.at, f32[520,256]{1,0:T(8,128)S(1)} %collective-permute-done.3.refs_0_.refs_4_, f32[3,4,512]{2,1,0:T(4,128)S(1)} %get-tuple-element.47.refs_1_, f32[20480,256]{1,0:T(8,128)S(1)} %get-tuple-element.44.refs_3_.refs_2_), custom_call_target="tpu_custom_call" | custom-call | bytes 15000000 | tf_op jit(solution)/shard_map/stats/pallas_call | solution.py:239
  45.7 3.9 %collective-permute-done.4.refs_1_ = f32[4,4,512]{2,1,0:T(4,128)S(1)} collective-permute-done((f32[4,4,512]{2,1,0:T(4,128)S(1)}, f32[4,4,512]{2,1,0:T(4,128)S(1)}, u32[]{:S(2)}, u32[]{:S(2)}) %collective-permute-start.4) | collective-permute-done | bytes 32800 | tf_op jit(solution)/shard_map/ppermute | solution.py:122
  50.1 3.8 %collective-permute-done.5 = f32[2,4,4,512]{3,2,1,0:T(4,128)S(1)} collective-permute-done((f32[2,4,4,512]{3,2,1,0:T(4,128)S(1)}, f32[2,4,4,512]{3,2,1,0:T(4,128)S(1)}, u32[]{:S(2)}, u32[]{:S(2)}) %collective-permute-start.5) | collective-permute-done | bytes 65568 | tf_op jit(solution)/shard_map/ppermute | solution.py:122
  53.9 3.7 %collective-permute-start.12 = (f32[520,256]{1,0:T(8,128)S(1)}, f32[520,256]{1,0:T(8,128)S(1)}, u32[]{:S(2)}, u32[]{:S(2)}) collective-permute-start(f32[520,256]{1,0:T(8,128)S(1)} %collective-permute-done.refs_0_.refs_2_), channel_id=1, source_target_pairs={{0,8},{4,12},{8,0},{12,4},{16,24},{20,28},{24,16},{28,20},{1,9},{5... | collective-permute-start | bytes 1597448 | tf_op jit(solution)/shard_map/ppermute | solution.py:122
  57.7 1.9 %collective-permute-start.13 = (f32[520,256]{1,0:T(8,128)S(1)}, f32[520,256]{1,0:T(8,128)S(1)}, u32[]{:S(2)}, u32[]{:S(2)}) collective-permute-start(f32[520,256]{1,0:T(8,128)S(1)} %collective-permute-done.9.refs_2_), channel_id=1, source_target_pairs={{0,1},{1,0},{2,3},{3,2},{4,5},{5,4},{6,7},{7,6},{8,9},{9,8},{10,11... | collective-permute-start | bytes 1597448 | tf_op jit(solution)/shard_map/ppermute | solution.py:122
  59.6 1.1 dq.1
  60.7 5.1 %item_grads.4 = (f32[5120,256]{1,0:T(8,128)S(1)}, f32[1,128]{1,0:T(1,128)S(1)}, f32[5120,256]{1,0:T(8,128)S(1)}, f32[2,512,256]{2,1,0:T(8,128)S(1)}) custom-call(s32[6]{0:T(128)S(1)} %stack.41.at, f32[2,4,512]{2,1,0:T(4,128)S(1)} %get-tuple-element.60.refs_0_.refs_6_, f32[520,256]{1,0:T(8,128)S(1)} %pack.1.refs_0_.refs_1_, ...), custom_call_target="tpu_custom_call", output_to_operand_aliasing={{3}: (6, {})} | custom-call | bytes 24000000 | tf_op jit(solution)/shard_map/item_grads/pallas_call | solution.py:395
  65.8 4.2 %collective-permute-start.10 = (f32[2,512,256]{2,1,0:T(8,128)S(1)}, f32[2,512,256]{2,1,0:T(8,128)S(1)}, u32[]{:S(2)}, u32[]{:S(2)}) collective-permute-start(f32[2,512,256]{2,1,0:T(8,128)S(1)} %get-tuple-element.62), channel_id=1, source_target_pairs={{0,1},{1,0},{2,3},{3,2},{4,5},{5,4},{6,7},{7,6},{8,9},{9,8},{10,11... | collective-permute-start | bytes 3145736 | tf_op jit(solution)/shard_map/ppermute | solution.py:122
  70.0 5.8 %collective-permute-start.11 = (f32[2,4,512]{2,1,0:T(4,128)S(1)}, f32[2,4,512]{2,1,0:T(4,128)S(1)}, u32[]{:S(2)}, u32[]{:S(2)}) collective-permute-start(f32[2,4,512]{2,1,0:T(4,128)S(1)} %get-tuple-element.60.refs_0_.refs_6_), channel_id=1, source_target_pairs={{0,8},{4,12},{8,0},{12,4},{16,24},{20,28},{24,16},{28,20},{1,9},{5... | collective-permute-start | bytes 49160 | tf_op jit(solution)/shard_map/ppermute | solution.py:122
  77.0 3.2 %collective-permute-start.16 = (f32[520,256]{1,0:T(8,128)S(1)}, f32[520,256]{1,0:T(8,128)S(1)}, u32[]{:S(2)}, u32[]{:S(2)}) collective-permute-start(f32[520,256]{1,0:T(8,128)S(1)} %collective-permute-done.6.refs_2_), channel_id=1, source_target_pairs={{0,2},{1,3},{2,0},{3,1},{4,6},{5,7},{6,4},{7,5},{8,10},{9,11},{10,... | collective-permute-start | bytes 1597448 | tf_op jit(solution)/shard_map/ppermute | solution.py:122
  82.6 1.5 %collective-permute-start.19 = (f32[520,256]{1,0:T(8,128)S(1)}, f32[520,256]{1,0:T(8,128)S(1)}, u32[]{:S(2)}, u32[]{:S(2)}) collective-permute-start(f32[520,256]{1,0:T(8,128)S(1)} %collective-permute-done.13.refs_3_), channel_id=1, source_target_pairs={{0,2},{1,3},{2,0},{3,1},{4,6},{5,7},{6,4},{7,5},{8,10},{9,11},{10,... | collective-permute-start | bytes 1597448 | tf_op jit(solution)/shard_map/ppermute | solution.py:122
  84.0 3.3 %collective-permute-done.15 = f32[2,2,4,512]{3,2,1,0:T(4,128)S(1)} collective-permute-done((f32[2,2,4,512]{3,2,1,0:T(4,128)S(1)}, f32[2,2,4,512]{3,2,1,0:T(4,128)S(1)}, u32[]{:S(2)}, u32[]{:S(2)}) %collective-permute-start.15) | collective-permute-done | bytes 32800 | tf_op jit(solution)/shard_map/ppermute | solution.py:122
  88.7 4.5 %collective-permute-done.16.refs_4_ = f32[520,256]{1,0:T(8,128)S(1)} collective-permute-done((f32[520,256]{1,0:T(8,128)S(1)}, f32[520,256]{1,0:T(8,128)S(1)}, u32[]{:S(2)}, u32[]{:S(2)}) %collective-permute-start.16) | collective-permute-done | bytes 532512 | tf_op jit(solution)/shard_map/ppermute | solution.py:122
  93.1 5.4 %item_grads.5 = (f32[5120,256]{1,0:T(8,128)S(1)}, f32[1,128]{1,0:T(1,128)S(1)}) custom-call(s32[6]{0:T(128)S(1)} %stack.41.at, f32[2,4,512]{2,1,0:T(4,128)S(1)} %get-tuple-element.78.refs_0_.refs_5_, f32[520,256]{1,0:T(8,128)S(1)} %collective-permute-done.2.refs_1_, f32[520,256]{1,0:T(8,128)S(1)} %collective-permute-done.6.refs_2_, ...), custom_call_target="tpu_custom_call", output_to_operand_aliasing={{0}: (8, {})} | custom-call | bytes 24000000 | tf_op jit(solution)/shard_map/item_grads/pallas_call | solution.py:395
  98.8 5.2 %collective-permute-start.17 = (f32[1,512,256]{2,1,0:T(8,128)S(1)}, f32[1,512,256]{2,1,0:T(8,128)S(1)}, u32[]{:S(2)}, u32[]{:S(2)}) collective-permute-start(f32[1,512,256]{2,1,0:T(8,128)S(1)} %slice.58), channel_id=1, source_target_pairs={{0,2},{1,3},{2,0},{3,1},{4,6},{5,7},{6,4},{7,5},{8,10},{9,11},{10,... | collective-permute-start | bytes 1572872 | tf_op jit(solution)/shard_map/ppermute | solution.py:122
  104.0 1.7 %collective-permute-start.18 = (f32[520,256]{1,0:T(8,128)S(1)}, f32[520,256]{1,0:T(8,128)S(1)}, u32[]{:S(2)}, u32[]{:S(2)}) collective-permute-start(f32[520,256]{1,0:T(8,128)S(1)} %broadcast_add_fusion.1), channel_id=1, source_target_pairs={{0,8},{4,12},{8,0},{12,4},{16,24},{20,28},{24,16},{28,20},{1,9},{5... | collective-permute-start | bytes 1597448 | tf_op jit(solution)/shard_map/ppermute | solution.py:122
  105.8 13.6 %item_grads.6 = (f32[5120,256]{1,0:T(8,128)S(1)}, f32[1,128]{1,0:T(1,128)}) custom-call(s32[6]{0:T(128)S(1)} %stack.41.at, f32[2,4,512]{2,1,0:T(4,128)S(1)} %get-tuple-element.77.refs_0_.refs_10_, f32[2,4,512]{2,1,0:T(4,128)S(1)} %collective-permute-done.11.refs_1_.refs_11_.refs_0_.refs_3_, ...), custom_call_target="tpu_custom_call", output_to_operand_aliasing={{0}: (14, {})} | custom-call | bytes 42000000 | tf_op jit(solution)/shard_map/item_grads/pallas_call | solution.py:395
  119.5 4.9 %item_grads.7 = (f32[5120,256]{1,0:T(8,128)S(1)}, f32[1,128]{1,0:T(1,128)}, f32[2560,256]{1,0:T(8,128)S(1)}, f32[2560,256]{1,0:T(8,128)S(1)}) custom-call(s32[6]{0:T(128)S(1)} %stack.41.at, f32[2,4,512]{2,1,0:T(4,128)S(1)} %collective-permute-done.11.refs_1_.refs_11_.refs_0_.refs_3_, ...), custom_call_target="tpu_custom_call", output_to_operand_aliasing={{0}: (6, {})} | custom-call | bytes 6000000 | tf_op jit(solution)/shard_map/item_grads/pallas_call | solution.py:395
  124.5 4.9 %collective-permute-done.21 = f32[2560,256]{1,0:T(8,128)S(1)} collective-permute-done((f32[2560,256]{1,0:T(8,128)S(1)}, f32[2560,256]{1,0:T(8,128)S(1)}, u32[]{:S(2)}, u32[]{:S(2)}) %collective-permute-start.21) | collective-permute-done | bytes 2621472 | tf_op jit(solution)/shard_map/ppermute | solution.py:122
  129.4 1.8 %add.63 = f32[2560,256]{1,0:T(8,128)} add(f32[2560,256]{1,0:T(8,128)S(1)} %get-tuple-element.73, f32[2560,256]{1,0:T(8,128)S(1)} %collective-permute-done.21) | non-fusion elementwise | flops 655360 | bytes 7864320 | tf_op jit(solution)/shard_map/add | solution.py:497
  (43 shorter events, 6.1 us)
Async XLA Ops:
  1.4 0.7 copy-start.1
  2.1 0.7 copy-start.2
  4.4 17.6 %collective-permute-start = (f32[520,256]{1,0:T(8,128)S(1)}, f32[520,256]{1,0:T(8,128)S(1)}, u32[]{:S(2)}, u32[]{:S(2)}) collective-permute-start(f32[520,256]{1,0:T(8,128)S(1)} %pack.1.refs_0_.refs_1_), channel_id=1, source_target_pairs={{0,1},{1,0},{2,3},{3,2},{4,5},{5,4},{6,7},{7,6},{8,9},{9,8},{10,11... | collective-permute-start | bytes 1597448 | tf_op jit(solution)/shard_map/ppermute | solution.py:122
  7.4 14.6 %collective-permute-start.1 = (f32[520,256]{1,0:T(8,128)S(1)}, f32[520,256]{1,0:T(8,128)S(1)}, u32[]{:S(2)}, u32[]{:S(2)}) collective-permute-start(f32[520,256]{1,0:T(8,128)S(1)} %pack.1.refs_0_.refs_1_), channel_id=1, source_target_pairs={{0,2},{1,3},{2,0},{3,1},{4,6},{5,7},{6,4},{7,5},{8,10},{9,11},{10,... | collective-permute-start | bytes 1597448 | tf_op jit(solution)/shard_map/ppermute | solution.py:122
  8.9 25.7 %collective-permute-start.2 = (f32[520,256]{1,0:T(8,128)S(1)}, f32[520,256]{1,0:T(8,128)S(1)}, u32[]{:S(2)}, u32[]{:S(2)}) collective-permute-start(f32[520,256]{1,0:T(8,128)S(1)} %pack.1.refs_0_.refs_1_), channel_id=1, source_target_pairs={{0,16},{4,20},{8,24},{12,28},{16,0},{20,4},{24,8},{28,12},{1,17},{... | collective-permute-start | bytes 1597448 | tf_op jit(solution)/shard_map/ppermute | solution.py:122
  22.0 13.3 %collective-permute-start.3 = (f32[520,256]{1,0:T(8,128)S(1)}, f32[520,256]{1,0:T(8,128)S(1)}, u32[]{:S(2)}, u32[]{:S(2)}) collective-permute-start(f32[520,256]{1,0:T(8,128)S(1)} %collective-permute-done.refs_0_.refs_2_), channel_id=1, source_target_pairs={{0,2},{1,3},{2,0},{3,1},{4,6},{5,7},{6,4},{7,5},{8,10},{9,11},{10,... | collective-permute-start | bytes 1597448 | tf_op jit(solution)/shard_map/ppermute | solution.py:122
  22.8 34.8 %collective-permute-start.8 = (f32[520,256]{1,0:T(8,128)S(1)}, f32[520,256]{1,0:T(8,128)S(1)}, u32[]{:S(2)}, u32[]{:S(2)}) collective-permute-start(f32[520,256]{1,0:T(8,128)S(1)} %pack.1.refs_0_.refs_1_), channel_id=1, source_target_pairs={{0,8},{4,12},{8,0},{12,4},{16,24},{20,28},{24,16},{28,20},{1,9},{5... | collective-permute-start | bytes 1597448 | tf_op jit(solution)/shard_map/ppermute | solution.py:122
  35.2 22.4 %collective-permute-start.6 = (f32[520,256]{1,0:T(8,128)S(1)}, f32[520,256]{1,0:T(8,128)S(1)}, u32[]{:S(2)}, u32[]{:S(2)}) collective-permute-start(f32[520,256]{1,0:T(8,128)S(1)} %collective-permute-done.2.refs_1_), channel_id=1, source_target_pairs={{0,1},{1,0},{2,3},{3,2},{4,5},{5,4},{6,7},{7,6},{8,9},{9,8},{10,11... | collective-permute-start | bytes 1597448 | tf_op jit(solution)/shard_map/ppermute | solution.py:122
  35.9 21.7 %collective-permute-start.7 = (f32[520,256]{1,0:T(8,128)S(1)}, f32[520,256]{1,0:T(8,128)S(1)}, u32[]{:S(2)}, u32[]{:S(2)}) collective-permute-start(f32[520,256]{1,0:T(8,128)S(1)} %collective-permute-done.2.refs_1_), channel_id=1, source_target_pairs={{0,2},{1,3},{2,0},{3,1},{4,6},{5,7},{6,4},{7,5},{8,10},{9,11},{10,... | collective-permute-start | bytes 1597448 | tf_op jit(solution)/shard_map/ppermute | solution.py:122
  38.7 19.0 %collective-permute-start.9 = (f32[520,256]{1,0:T(8,128)S(1)}, f32[520,256]{1,0:T(8,128)S(1)}, u32[]{:S(2)}, u32[]{:S(2)}) collective-permute-start(f32[520,256]{1,0:T(8,128)S(1)} %pack.1.refs_0_.refs_1_), channel_id=1, source_target_pairs={{0,24},{4,28},{8,16},{12,20},{16,8},{20,12},{24,0},{28,4},{1,25},{... | collective-permute-start | bytes 1597448 | tf_op jit(solution)/shard_map/ppermute | solution.py:122
  45.6 4.0 %collective-permute-start.4 = (f32[4,4,512]{2,1,0:T(4,128)S(1)}, f32[4,4,512]{2,1,0:T(4,128)S(1)}, u32[]{:S(2)}, u32[]{:S(2)}) collective-permute-start(f32[4,4,512]{2,1,0:T(4,128)S(1)} %get-tuple-element.48.refs_0_), channel_id=1, source_target_pairs={{0,1},{1,0},{2,3},{3,2},{4,5},{5,4},{6,7},{7,6},{8,9},{9,8},{10,11... | collective-permute-start | bytes 98312 | tf_op jit(solution)/shard_map/ppermute | solution.py:122
  49.6 4.3 %collective-permute-start.5 = (f32[2,4,4,512]{3,2,1,0:T(4,128)S(1)}, f32[2,4,4,512]{3,2,1,0:T(4,128)S(1)}, u32[]{:S(2)}, u32[]{:S(2)}) collective-permute-start(f32[2,4,4,512]{3,2,1,0:T(4,128)S(1)} %pad_maximum_fusion), channel_id=1, source_target_pairs={{0,2},{1,3},{2,0},{3,1},{4,6},{5,7},{6,4},{7,5},{8,10},{9,11},{10,... | collective-permute-start | bytes 196616 | tf_op jit(solution)/shard_map/ppermute | solution.py:122
  53.9 21.8 %collective-permute-start.12 = (f32[520,256]{1,0:T(8,128)S(1)}, f32[520,256]{1,0:T(8,128)S(1)}, u32[]{:S(2)}, u32[]{:S(2)}) collective-permute-start(f32[520,256]{1,0:T(8,128)S(1)} %collective-permute-done.refs_0_.refs_2_), channel_id=1, source_target_pairs={{0,8},{4,12},{8,0},{12,4},{16,24},{20,28},{24,16},{28,20},{1,9},{5... | collective-permute-start | bytes 1597448 | tf_op jit(solution)/shard_map/ppermute | solution.py:122
  57.7 22.5 %collective-permute-start.13 = (f32[520,256]{1,0:T(8,128)S(1)}, f32[520,256]{1,0:T(8,128)S(1)}, u32[]{:S(2)}, u32[]{:S(2)}) collective-permute-start(f32[520,256]{1,0:T(8,128)S(1)} %collective-permute-done.9.refs_2_), channel_id=1, source_target_pairs={{0,1},{1,0},{2,3},{3,2},{4,5},{5,4},{6,7},{7,6},{8,9},{9,8},{10,11... | collective-permute-start | bytes 1597448 | tf_op jit(solution)/shard_map/ppermute | solution.py:122
  59.6 21.7 %collective-permute-start.14 = (f32[520,256]{1,0:T(8,128)S(1)}, f32[520,256]{1,0:T(8,128)S(1)}, u32[]{:S(2)}, u32[]{:S(2)}) collective-permute-start(f32[520,256]{1,0:T(8,128)S(1)} %collective-permute-done.9.refs_2_), channel_id=1, source_target_pairs={{0,2},{1,3},{2,0},{3,1},{4,6},{5,7},{6,4},{7,5},{8,10},{9,11},{10,... | collective-permute-start | bytes 1597448 | tf_op jit(solution)/shard_map/ppermute | solution.py:122
  65.8 32.7 %collective-permute-start.10 = (f32[2,512,256]{2,1,0:T(8,128)S(1)}, f32[2,512,256]{2,1,0:T(8,128)S(1)}, u32[]{:S(2)}, u32[]{:S(2)}) collective-permute-start(f32[2,512,256]{2,1,0:T(8,128)S(1)} %get-tuple-element.62), channel_id=1, source_target_pairs={{0,1},{1,0},{2,3},{3,2},{4,5},{5,4},{6,7},{7,6},{8,9},{9,8},{10,11... | collective-permute-start | bytes 3145736 | tf_op jit(solution)/shard_map/ppermute | solution.py:122
  70.0 12.5 %collective-permute-start.11 = (f32[2,4,512]{2,1,0:T(4,128)S(1)}, f32[2,4,512]{2,1,0:T(4,128)S(1)}, u32[]{:S(2)}, u32[]{:S(2)}) collective-permute-start(f32[2,4,512]{2,1,0:T(4,128)S(1)} %get-tuple-element.60.refs_0_.refs_6_), channel_id=1, source_target_pairs={{0,8},{4,12},{8,0},{12,4},{16,24},{20,28},{24,16},{28,20},{1,9},{5... | collective-permute-start | bytes 49160 | tf_op jit(solution)/shard_map/ppermute | solution.py:122
  77.0 16.2 %collective-permute-start.16 = (f32[520,256]{1,0:T(8,128)S(1)}, f32[520,256]{1,0:T(8,128)S(1)}, u32[]{:S(2)}, u32[]{:S(2)}) collective-permute-start(f32[520,256]{1,0:T(8,128)S(1)} %collective-permute-done.6.refs_2_), channel_id=1, source_target_pairs={{0,2},{1,3},{2,0},{3,1},{4,6},{5,7},{6,4},{7,5},{8,10},{9,11},{10,... | collective-permute-start | bytes 1597448 | tf_op jit(solution)/shard_map/ppermute | solution.py:122
  82.5 4.9 %collective-permute-start.15 = (f32[2,2,4,512]{3,2,1,0:T(4,128)S(1)}, f32[2,2,4,512]{3,2,1,0:T(4,128)S(1)}, u32[]{:S(2)}, u32[]{:S(2)}) collective-permute-start(f32[2,2,4,512]{3,2,1,0:T(4,128)S(1)} %maximum_add_fusion), channel_id=1, source_target_pairs={{0,16},{4,20},{8,24},{12,28},{16,0},{20,4},{24,8},{28,12},{1,17},{... | collective-permute-start | bytes 98312 | tf_op jit(solution)/shard_map/ppermute | solution.py:122
  82.6 23.2 %collective-permute-start.19 = (f32[520,256]{1,0:T(8,128)S(1)}, f32[520,256]{1,0:T(8,128)S(1)}, u32[]{:S(2)}, u32[]{:S(2)}) collective-permute-start(f32[520,256]{1,0:T(8,128)S(1)} %collective-permute-done.13.refs_3_), channel_id=1, source_target_pairs={{0,2},{1,3},{2,0},{3,1},{4,6},{5,7},{6,4},{7,5},{8,10},{9,11},{10,... | collective-permute-start | bytes 1597448 | tf_op jit(solution)/shard_map/ppermute | solution.py:122
  88.6 17.2 %collective-permute-start.20 = (f32[520,256]{1,0:T(8,128)S(1)}, f32[520,256]{1,0:T(8,128)S(1)}, u32[]{:S(2)}, u32[]{:S(2)}) collective-permute-start(f32[520,256]{1,0:T(8,128)S(1)} %broadcast_add_fusion), channel_id=1, source_target_pairs={{0,8},{4,12},{8,0},{12,4},{16,24},{20,28},{24,16},{28,20},{1,9},{5... | collective-permute-start | bytes 1597448 | tf_op jit(solution)/shard_map/ppermute | solution.py:122
  98.8 20.6 %collective-permute-start.17 = (f32[1,512,256]{2,1,0:T(8,128)S(1)}, f32[1,512,256]{2,1,0:T(8,128)S(1)}, u32[]{:S(2)}, u32[]{:S(2)}) collective-permute-start(f32[1,512,256]{2,1,0:T(8,128)S(1)} %slice.58), channel_id=1, source_target_pairs={{0,2},{1,3},{2,0},{3,1},{4,6},{5,7},{6,4},{7,5},{8,10},{9,11},{10,... | collective-permute-start | bytes 1572872 | tf_op jit(solution)/shard_map/ppermute | solution.py:122
  104.0 15.4 %collective-permute-start.18 = (f32[520,256]{1,0:T(8,128)S(1)}, f32[520,256]{1,0:T(8,128)S(1)}, u32[]{:S(2)}, u32[]{:S(2)}) collective-permute-start(f32[520,256]{1,0:T(8,128)S(1)} %broadcast_add_fusion.1), channel_id=1, source_target_pairs={{0,8},{4,12},{8,0},{12,4},{16,24},{20,28},{24,16},{28,20},{1,9},{5... | collective-permute-start | bytes 1597448 | tf_op jit(solution)/shard_map/ppermute | solution.py:122
  119.5 4.9 %copy-start = (f32[512,256]{1,0:T(8,128)}, f32[512,256]{1,0:T(8,128)S(1)}, u32[]{:S(2)}) copy-start(f32[512,256]{1,0:T(8,128)S(1)} %fusion.refs_2_) | copy-start | bytes 1572868
  124.4 5.0 %collective-permute-start.21 = (f32[2560,256]{1,0:T(8,128)S(1)}, f32[2560,256]{1,0:T(8,128)S(1)}, u32[]{:S(2)}, u32[]{:S(2)}) collective-permute-start(f32[2560,256]{1,0:T(8,128)S(1)} %get-tuple-element.74), channel_id=1, source_target_pairs={{0,4},{4,0},{8,12},{12,8},{16,20},{20,16},{24,28},{28,24},{1,5},{5... | collective-permute-start | bytes 7864328 | tf_op jit(solution)/shard_map/ppermute | solution.py:122
where the time goes:
time: 132 us; the launch traced here: 131 us
  Pallas kernels  57.9 us (44%)
  starting transfers between devices  41.3 us (31%)
  waiting for transfers between devices  22 us (17%)
  local copies, waits for them, and re-layouts  4.29 us (3%)
  between operations  3.56 us (3%)
  other arithmetic  2.2 us (2%)
    ppermute x22, starting transfers between devices, swap(): lax.ppermute(x, axis, [(i, i ^ bits) for i in range(lax.axis_size(axis))])  41.3 us
    pallas_call x4, Pallas kernels, item_grads(): pl.pallas_call(functools.partial(item_kernel, sizes, lax.axis_size('shard...  28.9 us
    pallas_call x3, Pallas kernels, stats(): pl.pallas_call(functools.partial(stats_kernel, n, len(befores), lax.axis_...  26.3 us
    ppermute x22, waiting for transfers between devices, swap(): lax.ppermute(x, axis, [(i, i ^ bits) for i in range(lax.axis_size(axis))])  22 us
  transfers between devices with their start and end apart: 22, of which 7 were waited for; matrix products, arithmetic and copies ran while one was open for 2% of the time, Pallas kernels for 39%

commit v1 on v0

--- a/solution.py
+++ b/solution.py
@@ -480,7 +480,7 @@
             far[k].append(swap(far[k][j ^ top(j)], "shard", top(j)))
     grads, token = item_grads([(far[2], 0)], [terms[2]], chip_items, grads, span_rows, at, False)[:2]
 
-    shares = even + swap(odd, "shard", 1) + none(token)
+    shares = even + swap(odd, "shard", 1)
     half_way = shares
     bit = 2
     while bit < n_shard:

time: 132 us -> 141 us (1.068)
  the two profiles are of different devices: /device:TPU:0 before, /device:TPU:5 now
where the time goes in v1:
time: 141 us; the launch traced here: 139 us
  Pallas kernels  74.9 us (53%)
  waiting for transfers between devices  27.6 us (20%)
  starting transfers between devices  26.7 us (19%)
  local copies, waits for them, and re-layouts  4.29 us (3%)
  between operations  3.57 us (3%)
  other arithmetic  2.14 us (2%)
    pallas_call x4, Pallas kernels, item_grads(): pl.pallas_call(functools.partial(item_kernel, sizes, lax.axis_size('shard...  44.6 us
    ppermute x22, waiting for transfers between devices, swap(): lax.ppermute(x, axis, [(i, i ^ bits) for i in range(lax.axis_size(axis))])  27.6 us
    pallas_call x3, Pallas kernels, stats(): pl.pallas_call(functools.partial(stats_kernel, n, len(befores), lax.axis_...  27.5 us
    ppermute x22, starting transfers between devices, swap(): lax.ppermute(x, axis, [(i, i ^ bits) for i in range(lax.axis_size(axis))])  26.7 us
  transfers between devices with their start and end apart: 22, of which 6 were waited for; matrix products, arithmetic and copies ran while one was open for 2% of the time, Pallas kernels for 49%

profile of v1, /device:TPU:5, one launch (start us, length us, event | category | flops | bytes accessed | tf_op | source)
XLA Modules:
  0.0 139.1 jit_solution(14320296101118289755)
XLA Ops:
  0.6 0.8 copy.12.ids_ref
  1.4 0.7 copy-done.1
  2.1 0.7 copy-done.2
  2.7 1.6 %pack.1.refs_0_.refs_1_ = f32[520,256]{1,0:T(8,128)S(1)} custom-call(s32[1,4,3]{2,1,0:T(4,128)S(1)} %copy.12.ids_ref, s32[1,4]{1,0:T(1,128)S(1)} %copy-done.2, f32[512,256]{1,0:T(8,128)} %q_ref.1, s32[1,512]{1,0:T(1,128)S(1)} %bitcast.28), custom_call_target="tpu_custom_call" | custom-call | bytes 6000000 | tf_op jit(solution)/shard_map/pack/pallas_call | solution.py:83
  4.4 1.3 collective-permute-start
  5.9 2.3 %collective-permute-start.2 = (f32[520,256]{1,0:T(8,128)S(1)}, f32[520,256]{1,0:T(8,128)S(1)}, u32[]{:S(2)}, u32[]{:S(2)}) collective-permute-start(f32[520,256]{1,0:T(8,128)S(1)} %pack.1.refs_0_.refs_1_), channel_id=1, source_target_pairs={{0,16},{4,20},{8,24},{12,28},{16,0},{20,4},{24,8},{28,12},{1,17},{... | collective-permute-start | bytes 1597448 | tf_op jit(solution)/shard_map/ppermute | solution.py:122
  8.3 10.3 %stats.3 = (f32[1,256,512]{2,1,0:T(8,128)S(1)}, f32[1,256,512]{2,1,0:T(8,128)S(1)}, f32[1,4,512]{2,1,0:T(4,128)S(1)}, f32[20480,256]{1,0:T(8,128)S(1)}) custom-call(s32[6]{0:T(128)S(1)} %stack.41.at, f32[520,256]{1,0:T(8,128)S(1)} %pack.1.refs_0_.refs_1_, f32[20480,256]{1,0:T(8,128)} %refs_7_.1), custom_call_target="tpu_custom_call" | custom-call | bytes 15000000 | tf_op jit(solution)/shard_map/stats/pallas_call | solution.py:239
  18.6 1.5 %collective-permute-start.3 = (f32[520,256]{1,0:T(8,128)S(1)}, f32[520,256]{1,0:T(8,128)S(1)}, u32[]{:S(2)}, u32[]{:S(2)}) collective-permute-start(f32[520,256]{1,0:T(8,128)S(1)} %collective-permute-done.refs_0_.refs_2_), channel_id=1, source_target_pairs={{0,2},{1,3},{2,0},{3,1},{4,6},{5,7},{6,4},{7,5},{8,10},{9,11},{10,... | collective-permute-start | bytes 1597448 | tf_op jit(solution)/shard_map/ppermute | solution.py:122
  20.1 1.1 collective-permute-start.8
  21.2 12.4 %stats.4 = (f32[2,256,512]{2,1,0:T(8,128)S(1)}, f32[2,256,512]{2,1,0:T(8,128)S(1)}, f32[3,4,512]{2,1,0:T(4,128)S(1)}) custom-call(s32[6]{0:T(128)S(1)} %stack.41.at, f32[520,256]{1,0:T(8,128)S(1)} %collective-permute-done.refs_0_.refs_2_, f32[520,256]{1,0:T(8,128)S(1)} %collective-permute-done.1.refs_1_.refs_3_, f32[1,4,512]{2,1,0:T(4,128)S(1)} %get-tuple-element.42.refs_2_, ...), custom_call_target="tpu_custom_call" | custom-call | bytes 30000000 | tf_op jit(solution)/shard_map/stats/pallas_call | solution.py:239
  33.7 1.9 %collective-permute-start.6 = (f32[520,256]{1,0:T(8,128)S(1)}, f32[520,256]{1,0:T(8,128)S(1)}, u32[]{:S(2)}, u32[]{:S(2)}) collective-permute-start(f32[520,256]{1,0:T(8,128)S(1)} %collective-permute-done.2.refs_1_), channel_id=1, source_target_pairs={{0,1},{1,0},{2,3},{3,2},{4,5},{5,4},{6,7},{7,6},{8,9},{9,8},{10,11... | collective-permute-start | bytes 1597448 | tf_op jit(solution)/shard_map/ppermute | solution.py:122
  35.6 1.8 %collective-permute-start.9 = (f32[520,256]{1,0:T(8,128)S(1)}, f32[520,256]{1,0:T(8,128)S(1)}, u32[]{:S(2)}, u32[]{:S(2)}) collective-permute-start(f32[520,256]{1,0:T(8,128)S(1)} %pack.1.refs_0_.refs_1_), channel_id=1, source_target_pairs={{0,24},{4,28},{8,16},{12,20},{16,8},{20,12},{24,0},{28,4},{1,25},{... | collective-permute-start | bytes 1597448 | tf_op jit(solution)/shard_map/ppermute | solution.py:122
  37.4 4.8 %stats.5 = (f32[1,256,512]{2,1,0:T(8,128)S(1)}, f32[1,256,512]{2,1,0:T(8,128)S(1)}, f32[4,4,512]{2,1,0:T(4,128)S(1)}) custom-call(s32[6]{0:T(128)S(1)} %stack.41.at, f32[520,256]{1,0:T(8,128)S(1)} %collective-permute-done.3.refs_0_.refs_4_, f32[3,4,512]{2,1,0:T(4,128)S(1)} %get-tuple-element.46.refs_1_, f32[20480,256]{1,0:T(8,128)S(1)} %get-tuple-element.43.refs_3_.refs_2_), custom_call_target="tpu_custom_call" | custom-call | bytes 15000000 | tf_op jit(solution)/shard_map/stats/pallas_call | solution.py:239
  42.3 2.1 %collective-permute-start.4 = (f32[4,4,512]{2,1,0:T(4,128)S(1)}, f32[4,4,512]{2,1,0:T(4,128)S(1)}, u32[]{:S(2)}, u32[]{:S(2)}) collective-permute-start(f32[4,4,512]{2,1,0:T(4,128)S(1)} %get-tuple-element.47.refs_0_), channel_id=1, source_target_pairs={{0,1},{1,0},{2,3},{3,2},{4,5},{5,4},{6,7},{7,6},{8,9},{9,8},{10,11... | collective-permute-start | bytes 98312 | tf_op jit(solution)/shard_map/ppermute | solution.py:122
  44.3 3.9 %collective-permute-done.4.refs_1_ = f32[4,4,512]{2,1,0:T(4,128)S(1)} collective-permute-done((f32[4,4,512]{2,1,0:T(4,128)S(1)}, f32[4,4,512]{2,1,0:T(4,128)S(1)}, u32[]{:S(2)}, u32[]{:S(2)}) %collective-permute-start.4) | collective-permute-done | bytes 32800 | tf_op jit(solution)/shard_map/ppermute | solution.py:122
  48.3 3.4 %collective-permute-done.5 = f32[2,4,4,512]{3,2,1,0:T(4,128)S(1)} collective-permute-done((f32[2,4,4,512]{3,2,1,0:T(4,128)S(1)}, f32[2,4,4,512]{3,2,1,0:T(4,128)S(1)}, u32[]{:S(2)}, u32[]{:S(2)}) %collective-permute-start.5) | collective-permute-done | bytes 65568 | tf_op jit(solution)/shard_map/ppermute | solution.py:122
  51.7 3.3 %collective-permute-done.8.refs_6_ = f32[520,256]{1,0:T(8,128)S(1)} collective-permute-done((f32[520,256]{1,0:T(8,128)S(1)}, f32[520,256]{1,0:T(8,128)S(1)}, u32[]{:S(2)}, u32[]{:S(2)}) %collective-permute-start.8) | collective-permute-done | bytes 532512 | tf_op jit(solution)/shard_map/ppermute | solution.py:122
  55.3 0.9 collective-permute-start.15
  56.2 1.1 dq.1
  57.4 10.6 %item_grads.4 = (f32[5120,256]{1,0:T(8,128)S(1)}, f32[1,128]{1,0:T(1,128)S(1)}, f32[5120,256]{1,0:T(8,128)S(1)}, f32[2,512,256]{2,1,0:T(8,128)S(1)}) custom-call(s32[6]{0:T(128)S(1)} %stack.41.at, f32[2,4,512]{2,1,0:T(4,128)S(1)} %get-tuple-element.59.refs_0_.refs_6_, f32[520,256]{1,0:T(8,128)S(1)} %pack.1.refs_0_.refs_1_, ...), custom_call_target="tpu_custom_call", output_to_operand_aliasing={{3}: (6, {})} | custom-call | bytes 24000000 | tf_op jit(solution)/shard_map/item_grads/pallas_call | solution.py:395
  67.9 1.4 collective-permute-start.10
  69.3 4.4 %collective-permute-start.12 = (f32[2,4,512]{2,1,0:T(4,128)S(1)}, f32[2,4,512]{2,1,0:T(4,128)S(1)}, u32[]{:S(2)}, u32[]{:S(2)}) collective-permute-start(f32[2,4,512]{2,1,0:T(4,128)S(1)} %get-tuple-element.59.refs_0_.refs_6_), channel_id=1, source_target_pairs={{0,8},{4,12},{8,0},{12,4},{16,24},{20,28},{24,16},{28,20},{1,9},{5... | collective-permute-start | bytes 49160 | tf_op jit(solution)/shard_map/ppermute | solution.py:122
  77.5 1.5 %collective-permute-start.18 = (f32[520,256]{1,0:T(8,128)S(1)}, f32[520,256]{1,0:T(8,128)S(1)}, u32[]{:S(2)}, u32[]{:S(2)}) collective-permute-start(f32[520,256]{1,0:T(8,128)S(1)} %collective-permute-done.14.refs_3_), channel_id=1, source_target_pairs={{0,2},{1,3},{2,0},{3,1},{4,6},{5,7},{6,4},{7,5},{8,10},{9,11},{10,... | collective-permute-start | bytes 1597448 | tf_op jit(solution)/shard_map/ppermute | solution.py:122
  78.9 2.2 %collective-permute-done.16 = f32[2,2,4,512]{3,2,1,0:T(4,128)S(1)} collective-permute-done((f32[2,2,4,512]{3,2,1,0:T(4,128)S(1)}, f32[2,2,4,512]{3,2,1,0:T(4,128)S(1)}, u32[]{:S(2)}, u32[]{:S(2)}) %collective-permute-start.16) | collective-permute-done | bytes 32800 | tf_op jit(solution)/shard_map/ppermute | solution.py:122
  81.1 0.5 slice.55
  82.4 9.8 %collective-permute-done.10 = f32[2,512,256]{2,1,0:T(8,128)S(1)} collective-permute-done((f32[2,512,256]{2,1,0:T(8,128)S(1)}, f32[2,512,256]{2,1,0:T(8,128)S(1)}, u32[]{:S(2)}, u32[]{:S(2)}) %collective-permute-start.10) | collective-permute-done | bytes 1048608 | tf_op jit(solution)/shard_map/ppermute | solution.py:122
  92.6 5.5 %collective-permute-start.17 = (f32[520,256]{1,0:T(8,128)S(1)}, f32[520,256]{1,0:T(8,128)S(1)}, u32[]{:S(2)}, u32[]{:S(2)}) collective-permute-start(f32[520,256]{1,0:T(8,128)S(1)} %broadcast_add_fusion.1), channel_id=1, source_target_pairs={{0,8},{4,12},{8,0},{12,4},{16,24},{20,28},{24,16},{28,20},{1,9},{5... | collective-permute-start | bytes 1597448 | tf_op jit(solution)/shard_map/ppermute | solution.py:122
  98.1 12.6 %item_grads.5 = (f32[5120,256]{1,0:T(8,128)S(1)}, f32[1,128]{1,0:T(1,128)}) custom-call(s32[6]{0:T(128)S(1)} %stack.41.at, f32[2,4,512]{2,1,0:T(4,128)S(1)} %get-tuple-element.75.refs_0_.refs_5_, f32[520,256]{1,0:T(8,128)S(1)} %collective-permute-done.2.refs_1_, f32[520,256]{1,0:T(8,128)S(1)} %collective-permute-done.6.refs_2_, ...), custom_call_target="tpu_custom_call", output_to_operand_aliasing={{0}: (8, {})} | custom-call | bytes 24000000 | tf_op jit(solution)/shard_map/item_grads/pallas_call | solution.py:395
  110.7 16.7 %item_grads.6 = (f32[5120,256]{1,0:T(8,128)S(1)}, f32[1,128]{1,0:T(1,128)}) custom-call(s32[6]{0:T(128)S(1)} %stack.41.at, f32[2,4,512]{2,1,0:T(4,128)S(1)} %get-tuple-element.76.refs_0_.refs_10_, f32[2,4,512]{2,1,0:T(4,128)S(1)} %collective-permute-done.12.refs_1_.refs_11_.refs_0_.refs_3_, ...), custom_call_target="tpu_custom_call", output_to_operand_aliasing={{0}: (14, {})} | custom-call | bytes 42000000 | tf_op jit(solution)/shard_map/item_grads/pallas_call | solution.py:395
  127.5 4.8 %item_grads.7 = (f32[5120,256]{1,0:T(8,128)S(1)}, f32[1,128]{1,0:T(1,128)}, f32[2560,256]{1,0:T(8,128)S(1)}, f32[2560,256]{1,0:T(8,128)S(1)}) custom-call(s32[6]{0:T(128)S(1)} %stack.41.at, f32[2,4,512]{2,1,0:T(4,128)S(1)} %collective-permute-done.12.refs_1_.refs_11_.refs_0_.refs_3_, ...), custom_call_target="tpu_custom_call", output_to_operand_aliasing={{0}: (6, {})} | custom-call | bytes 6000000 | tf_op jit(solution)/shard_map/item_grads/pallas_call | solution.py:395
  132.4 4.9 %collective-permute-done.21 = f32[2560,256]{1,0:T(8,128)S(1)} collective-permute-done((f32[2560,256]{1,0:T(8,128)S(1)}, f32[2560,256]{1,0:T(8,128)S(1)}, u32[]{:S(2)}, u32[]{:S(2)}) %collective-permute-start.21) | collective-permute-done | bytes 2621472 | tf_op jit(solution)/shard_map/ppermute | solution.py:122
  137.3 1.8 %add.55 = f32[2560,256]{1,0:T(8,128)} add(f32[2560,256]{1,0:T(8,128)S(1)} %get-tuple-element.71, f32[2560,256]{1,0:T(8,128)S(1)} %collective-permute-done.21) | non-fusion elementwise | flops 655360 | bytes 7864320 | tf_op jit(solution)/shard_map/add | solution.py:497
  (43 shorter events, 3.0 us)
Async XLA Ops:
  1.4 0.7 copy-start.1
  2.1 0.7 copy-start.2
  4.4 14.2 %collective-permute-start = (f32[520,256]{1,0:T(8,128)S(1)}, f32[520,256]{1,0:T(8,128)S(1)}, u32[]{:S(2)}, u32[]{:S(2)}) collective-permute-start(f32[520,256]{1,0:T(8,128)S(1)} %pack.1.refs_0_.refs_1_), channel_id=1, source_target_pairs={{0,1},{1,0},{2,3},{3,2},{4,5},{5,4},{6,7},{7,6},{8,9},{9,8},{10,11... | collective-permute-start | bytes 1597448 | tf_op jit(solution)/shard_map/ppermute | solution.py:122
  5.6 12.9 %collective-permute-start.1 = (f32[520,256]{1,0:T(8,128)S(1)}, f32[520,256]{1,0:T(8,128)S(1)}, u32[]{:S(2)}, u32[]{:S(2)}) collective-permute-start(f32[520,256]{1,0:T(8,128)S(1)} %pack.1.refs_0_.refs_1_), channel_id=1, source_target_pairs={{0,2},{1,3},{2,0},{3,1},{4,6},{5,7},{6,4},{7,5},{8,10},{9,11},{10,... | collective-permute-start | bytes 1597448 | tf_op jit(solution)/shard_map/ppermute | solution.py:122
  5.9 27.8 %collective-permute-start.2 = (f32[520,256]{1,0:T(8,128)S(1)}, f32[520,256]{1,0:T(8,128)S(1)}, u32[]{:S(2)}, u32[]{:S(2)}) collective-permute-start(f32[520,256]{1,0:T(8,128)S(1)} %pack.1.refs_0_.refs_1_), channel_id=1, source_target_pairs={{0,16},{4,20},{8,24},{12,28},{16,0},{20,4},{24,8},{28,12},{1,17},{... | collective-permute-start | bytes 1597448 | tf_op jit(solution)/shard_map/ppermute | solution.py:122
  18.6 15.1 %collective-permute-start.3 = (f32[520,256]{1,0:T(8,128)S(1)}, f32[520,256]{1,0:T(8,128)S(1)}, u32[]{:S(2)}, u32[]{:S(2)}) collective-permute-start(f32[520,256]{1,0:T(8,128)S(1)} %collective-permute-done.refs_0_.refs_2_), channel_id=1, source_target_pairs={{0,2},{1,3},{2,0},{3,1},{4,6},{5,7},{6,4},{7,5},{8,10},{9,11},{10,... | collective-permute-start | bytes 1597448 | tf_op jit(solution)/shard_map/ppermute | solution.py:122
  20.1 34.9 %collective-permute-start.8 = (f32[520,256]{1,0:T(8,128)S(1)}, f32[520,256]{1,0:T(8,128)S(1)}, u32[]{:S(2)}, u32[]{:S(2)}) collective-permute-start(f32[520,256]{1,0:T(8,128)S(1)} %pack.1.refs_0_.refs_1_), channel_id=1, source_target_pairs={{0,8},{4,12},{8,0},{12,4},{16,24},{20,28},{24,16},{28,20},{1,9},{5... | collective-permute-start | bytes 1597448 | tf_op jit(solution)/shard_map/ppermute | solution.py:122
  33.7 21.4 %collective-permute-start.6 = (f32[520,256]{1,0:T(8,128)S(1)}, f32[520,256]{1,0:T(8,128)S(1)}, u32[]{:S(2)}, u32[]{:S(2)}) collective-permute-start(f32[520,256]{1,0:T(8,128)S(1)} %collective-permute-done.2.refs_1_), channel_id=1, source_target_pairs={{0,1},{1,0},{2,3},{3,2},{4,5},{5,4},{6,7},{7,6},{8,9},{9,8},{10,11... | collective-permute-start | bytes 1597448 | tf_op jit(solution)/shard_map/ppermute | solution.py:122
  35.6 19.4 %collective-permute-start.7 = (f32[520,256]{1,0:T(8,128)S(1)}, f32[520,256]{1,0:T(8,128)S(1)}, u32[]{:S(2)}, u32[]{:S(2)}) collective-permute-start(f32[520,256]{1,0:T(8,128)S(1)} %collective-permute-done.2.refs_1_), channel_id=1, source_target_pairs={{0,2},{1,3},{2,0},{3,1},{4,6},{5,7},{6,4},{7,5},{8,10},{9,11},{10,... | collective-permute-start | bytes 1597448 | tf_op jit(solution)/shard_map/ppermute | solution.py:122
  35.6 19.4 %collective-permute-start.9 = (f32[520,256]{1,0:T(8,128)S(1)}, f32[520,256]{1,0:T(8,128)S(1)}, u32[]{:S(2)}, u32[]{:S(2)}) collective-permute-start(f32[520,256]{1,0:T(8,128)S(1)} %pack.1.refs_0_.refs_1_), channel_id=1, source_target_pairs={{0,24},{4,28},{8,16},{12,20},{16,8},{20,12},{24,0},{28,4},{1,25},{... | collective-permute-start | bytes 1597448 | tf_op jit(solution)/shard_map/ppermute | solution.py:122
  42.3 5.9 %collective-permute-start.4 = (f32[4,4,512]{2,1,0:T(4,128)S(1)}, f32[4,4,512]{2,1,0:T(4,128)S(1)}, u32[]{:S(2)}, u32[]{:S(2)}) collective-permute-start(f32[4,4,512]{2,1,0:T(4,128)S(1)} %get-tuple-element.47.refs_0_), channel_id=1, source_target_pairs={{0,1},{1,0},{2,3},{3,2},{4,5},{5,4},{6,7},{7,6},{8,9},{9,8},{10,11... | collective-permute-start | bytes 98312 | tf_op jit(solution)/shard_map/ppermute | solution.py:122
  48.2 3.5 %collective-permute-start.5 = (f32[2,4,4,512]{3,2,1,0:T(4,128)S(1)}, f32[2,4,4,512]{3,2,1,0:T(4,128)S(1)}, u32[]{:S(2)}, u32[]{:S(2)}) collective-permute-start(f32[2,4,4,512]{3,2,1,0:T(4,128)S(1)} %pad_maximum_fusion), channel_id=1, source_target_pairs={{0,2},{1,3},{2,0},{3,1},{4,6},{5,7},{6,4},{7,5},{8,10},{9,11},{10,... | collective-permute-start | bytes 196616 | tf_op jit(solution)/shard_map/ppermute | solution.py:122
  51.7 22.0 %collective-permute-start.13 = (f32[520,256]{1,0:T(8,128)S(1)}, f32[520,256]{1,0:T(8,128)S(1)}, u32[]{:S(2)}, u32[]{:S(2)}) collective-permute-start(f32[520,256]{1,0:T(8,128)S(1)} %collective-permute-done.refs_0_.refs_2_), channel_id=1, source_target_pairs={{0,8},{4,12},{8,0},{12,4},{16,24},{20,28},{24,16},{28,20},{1,9},{5... | collective-permute-start | bytes 1597448 | tf_op jit(solution)/shard_map/ppermute | solution.py:122
  55.0 19.9 %collective-permute-start.14 = (f32[520,256]{1,0:T(8,128)S(1)}, f32[520,256]{1,0:T(8,128)S(1)}, u32[]{:S(2)}, u32[]{:S(2)}) collective-permute-start(f32[520,256]{1,0:T(8,128)S(1)} %collective-permute-done.9.refs_2_), channel_id=1, source_target_pairs={{0,1},{1,0},{2,3},{3,2},{4,5},{5,4},{6,7},{7,6},{8,9},{9,8},{10,11... | collective-permute-start | bytes 1597448 | tf_op jit(solution)/shard_map/ppermute | solution.py:122
  55.3 20.8 %collective-permute-start.15 = (f32[520,256]{1,0:T(8,128)S(1)}, f32[520,256]{1,0:T(8,128)S(1)}, u32[]{:S(2)}, u32[]{:S(2)}) collective-permute-start(f32[520,256]{1,0:T(8,128)S(1)} %collective-permute-done.9.refs_2_), channel_id=1, source_target_pairs={{0,2},{1,3},{2,0},{3,1},{4,6},{5,7},{6,4},{7,5},{8,10},{9,11},{10,... | collective-permute-start | bytes 1597448 | tf_op jit(solution)/shard_map/ppermute | solution.py:122
  67.9 24.3 %collective-permute-start.10 = (f32[2,512,256]{2,1,0:T(8,128)S(1)}, f32[2,512,256]{2,1,0:T(8,128)S(1)}, u32[]{:S(2)}, u32[]{:S(2)}) collective-permute-start(f32[2,512,256]{2,1,0:T(8,128)S(1)} %get-tuple-element.61), channel_id=1, source_target_pairs={{0,1},{1,0},{2,3},{3,2},{4,5},{5,4},{6,7},{7,6},{8,9},{9,8},{10,11... | collective-permute-start | bytes 3145736 | tf_op jit(solution)/shard_map/ppermute | solution.py:122
  69.3 8.0 %collective-permute-start.12 = (f32[2,4,512]{2,1,0:T(4,128)S(1)}, f32[2,4,512]{2,1,0:T(4,128)S(1)}, u32[]{:S(2)}, u32[]{:S(2)}) collective-permute-start(f32[2,4,512]{2,1,0:T(4,128)S(1)} %get-tuple-element.59.refs_0_.refs_6_), channel_id=1, source_target_pairs={{0,8},{4,12},{8,0},{12,4},{16,24},{20,28},{24,16},{28,20},{1,9},{5... | collective-permute-start | bytes 49160 | tf_op jit(solution)/shard_map/ppermute | solution.py:122
  77.3 3.8 %collective-permute-start.16 = (f32[2,2,4,512]{3,2,1,0:T(4,128)S(1)}, f32[2,2,4,512]{3,2,1,0:T(4,128)S(1)}, u32[]{:S(2)}, u32[]{:S(2)}) collective-permute-start(f32[2,2,4,512]{3,2,1,0:T(4,128)S(1)} %maximum_add_fusion), channel_id=1, source_target_pairs={{0,16},{4,20},{8,24},{12,28},{16,0},{20,4},{24,8},{28,12},{1,17},{... | collective-permute-start | bytes 98312 | tf_op jit(solution)/shard_map/ppermute | solution.py:122
  77.4 20.7 %collective-permute-start.20 = (f32[520,256]{1,0:T(8,128)S(1)}, f32[520,256]{1,0:T(8,128)S(1)}, u32[]{:S(2)}, u32[]{:S(2)}) collective-permute-start(f32[520,256]{1,0:T(8,128)S(1)} %collective-permute-done.6.refs_2_), channel_id=1, source_target_pairs={{0,2},{1,3},{2,0},{3,1},{4,6},{5,7},{6,4},{7,5},{8,10},{9,11},{10,... | collective-permute-start | bytes 1597448 | tf_op jit(solution)/shard_map/ppermute | solution.py:122
  77.5 33.2 %collective-permute-start.18 = (f32[520,256]{1,0:T(8,128)S(1)}, f32[520,256]{1,0:T(8,128)S(1)}, u32[]{:S(2)}, u32[]{:S(2)}) collective-permute-start(f32[520,256]{1,0:T(8,128)S(1)} %collective-permute-done.14.refs_3_), channel_id=1, source_target_pairs={{0,2},{1,3},{2,0},{3,1},{4,6},{5,7},{6,4},{7,5},{8,10},{9,11},{10,... | collective-permute-start | bytes 1597448 | tf_op jit(solution)/shard_map/ppermute | solution.py:122
  82.3 28.4 %collective-permute-start.19 = (f32[520,256]{1,0:T(8,128)S(1)}, f32[520,256]{1,0:T(8,128)S(1)}, u32[]{:S(2)}, u32[]{:S(2)}) collective-permute-start(f32[520,256]{1,0:T(8,128)S(1)} %broadcast_add_fusion), channel_id=1, source_target_pairs={{0,8},{4,12},{8,0},{12,4},{16,24},{20,28},{24,16},{28,20},{1,9},{5... | collective-permute-start | bytes 1597448 | tf_op jit(solution)/shard_map/ppermute | solution.py:122
  92.4 35.0 %collective-permute-start.11 = (f32[1,512,256]{2,1,0:T(8,128)S(1)}, f32[1,512,256]{2,1,0:T(8,128)S(1)}, u32[]{:S(2)}, u32[]{:S(2)}) collective-permute-start(f32[1,512,256]{2,1,0:T(8,128)S(1)} %slice.50), channel_id=1, source_target_pairs={{0,2},{1,3},{2,0},{3,1},{4,6},{5,7},{6,4},{7,5},{8,10},{9,11},{10,... | collective-permute-start | bytes 1572872 | tf_op jit(solution)/shard_map/ppermute | solution.py:122
  92.6 34.9 %collective-permute-start.17 = (f32[520,256]{1,0:T(8,128)S(1)}, f32[520,256]{1,0:T(8,128)S(1)}, u32[]{:S(2)}, u32[]{:S(2)}) collective-permute-start(f32[520,256]{1,0:T(8,128)S(1)} %broadcast_add_fusion.1), channel_id=1, source_target_pairs={{0,8},{4,12},{8,0},{12,4},{16,24},{20,28},{24,16},{28,20},{1,9},{5... | collective-permute-start | bytes 1597448 | tf_op jit(solution)/shard_map/ppermute | solution.py:122
  127.5 4.8 %copy-start = (f32[512,256]{1,0:T(8,128)}, f32[512,256]{1,0:T(8,128)S(1)}, u32[]{:S(2)}) copy-start(f32[512,256]{1,0:T(8,128)S(1)} %fusion.refs_2_) | copy-start | bytes 1572868
  132.3 5.0 %collective-permute-start.21 = (f32[2560,256]{1,0:T(8,128)S(1)}, f32[2560,256]{1,0:T(8,128)S(1)}, u32[]{:S(2)}, u32[]{:S(2)}) collective-permute-start(f32[2560,256]{1,0:T(8,128)S(1)} %get-tuple-element.72), channel_id=1, source_target_pairs={{0,4},{4,0},{8,12},{12,8},{16,20},{20,16},{24,28},{28,24},{1,5},{5... | collective-permute-start | bytes 7864328 | tf_op jit(solution)/shard_map/ppermute | solution.py:122
